TPU v7x, 32 devices: a whole 2x2x4 slice. The times are simulated.
32 devices in a mesh: row: 8 (over y, x, core), col: 4 (over z).
Axes of the slice: x: 2, y: 2, z: 4, core: 2. Of those that a mesh axis runs over, the one named last changes fastest.
Arguments:
- positions: bfloat16 [3, 49152], P(None, 'row'), may hold values from -3.3 to 3.3, as said below
- normals: bfloat16 [3, 49152], P(None, 'row'), may hold values from -1 to 1, as said below
- areas: bfloat16 [49152], P('row'), as said below
- radiosity: bfloat16 [32, 49152], P(None, 'row'), may hold values from 0.19921875 to 5
- reflect: float32 [49152], P('row'), may hold values from 0.2 to 0.9
- partial_sums: float32 [128, 49152], P('col', 'row'), may hold values from -6 to 6
- visible: int32 [384, 384], P('row'), may hold values 0 or 1
- section: int32 [1], replicated, may hold values from 0 to 7
Outputs:
- advanced: float32 [128, 49152], P('col', 'row')
Inputs may be any that keep to these rules, and one draw needn't show every extreme that they name: `positions`: patches of one block lie around a common centre. `normals`: each column has length close to 1. `areas`: each area is positive; 6144 times an area lies between 51 and 1640.
All inputs are finite; a program needn't handle non-finite values. No bound on the sum of `visible` on one device may be relied on, other than what follows from the above.
Results may differ from a plain program's by a relative error of at most 0.0003.
Values may be sent and summed in bfloat16 or wider, within the bound.
No kernel may reach another device: no remote copies, remote signals or barrier semaphores. Data moves between devices by JAX's collectives and lax.ppermute only.
A program may use at most 64 MiB of HBM per device.

v0:
```python
import math

import jax
import jax.numpy as jnp
from jax import lax
from jax.sharding import PartitionSpec as P


def from_root(shard, axis, root):
    mine = lax.axis_index(axis) == root
    return lax.psum(jnp.where(mine, shard, jnp.zeros_like(shard)), axis)


def shifted(block, axis, distance):
    devices = range(lax.axis_size(axis))
    route = [((i - distance) % len(devices), i) for i in devices]
    return lax.ppermute(block, axis, route)


def block_term(rec_pos, rec_nrm, em_pos, em_nrm, em_area, em_rad, mask_block):
    rows = rec_pos.shape[1]
    cols = em_pos.shape[1]
    row_block_size = min(1024, rows)
    column_block_size = min(2048, cols)
    rcount = rows // row_block_size
    ccount = cols // column_block_size
    cases = em_rad.shape[0]

    def one_block(index):
        start = index * row_block_size
        rpos = lax.dynamic_slice_in_dim(rec_pos, start, row_block_size, 1).astype(jnp.float32)
        rnrm = lax.dynamic_slice_in_dim(rec_nrm, start, row_block_size, 1).astype(jnp.float32)
        matrix_row_count = lax.dynamic_slice_in_dim(
            mask_block, index * (row_block_size // 128), row_block_size // 128, 0
        )

        def one_column(total, column_block_index):
            cstart = column_block_index * column_block_size
            epos = lax.dynamic_slice_in_dim(em_pos, cstart, column_block_size, 1).astype(
                jnp.float32
            )
            enrm = lax.dynamic_slice_in_dim(em_nrm, cstart, column_block_size, 1).astype(
                jnp.float32
            )
            earea = lax.dynamic_slice_in_dim(em_area, cstart, column_block_size, 0).astype(
                jnp.float32
            )
            erad = lax.dynamic_slice_in_dim(em_rad, cstart, column_block_size, 1)
            matrix_tile_block = lax.dynamic_slice_in_dim(
                matrix_row_count,
                column_block_index * (column_block_size // 128),
                column_block_size // 128,
                1,
            )
            delta_x = rpos[0][:, None] - epos[0][None, :]
            delta_y = rpos[1][:, None] - epos[1][None, :]
            delta_z = rpos[2][:, None] - epos[2][None, :]
            dist_sq = delta_x * delta_x + delta_y * delta_y + delta_z * delta_z
            emit_cos = jnp.maximum(
                enrm[0][None, :] * delta_x
                + enrm[1][None, :] * delta_y
                + enrm[2][None, :] * delta_z,
                0.0,
            )
            recv_cos = jnp.maximum(
                -(
                    rnrm[0][:, None] * delta_x
                    + rnrm[1][:, None] * delta_y
                    + rnrm[2][:, None] * delta_z
                ),
                0.0,
            )
            kernel = (
                emit_cos
                * recv_cos
                * earea[None, :]
                / ((dist_sq + earea[None, :]) * (math.pi * dist_sq + earea[None, :]))
            )
            receiver_tile_count = matrix_tile_block.shape[0]
            emitter_tile_count = matrix_tile_block.shape[1]
            visited_flags = jnp.broadcast_to(
                matrix_tile_block[:, None, :, None],
                (receiver_tile_count, 128, emitter_tile_count, 128),
            ).reshape(row_block_size, column_block_size)
            view = (kernel * visited_flags.astype(jnp.float32)).astype(jnp.bfloat16)
            return (total + jnp.dot(erad, view.T, preferred_element_type=jnp.float32), None)

        init = jnp.zeros((cases, row_block_size), jnp.float32)
        total, unused = lax.scan(one_column, init, jnp.arange(ccount, dtype=jnp.int32))
        return total

    parts = lax.map(one_block, jnp.arange(rcount, dtype=jnp.int32))
    return jnp.transpose(parts, (1, 0, 2)).reshape(cases, rows)


def section_term(positions, normals, areas, radiosity, visible, section, offset):
    n_row = lax.axis_size("row")
    n_col = lax.axis_size("col")
    block = positions.shape[1]
    tiles = block // 128
    column = lax.axis_index("col")
    emit = ((column + offset) % n_col + section[0]) % n_row
    em_pos, em_nrm, em_area, em_rad = (
        from_root(positions, "row", emit),
        from_root(normals, "row", emit),
        from_root(areas, "row", emit),
        from_root(radiosity, "row", emit),
    )
    mask_block = lax.dynamic_slice_in_dim(visible, emit * tiles, tiles, 1)
    return block_term(positions, normals, em_pos, em_nrm, em_area, em_rad, mask_block)


def on_device(positions, normals, areas, radiosity, reflect, partial_sums, visible, section):
    term = section_term(positions, normals, areas, radiosity, visible, section, 1)
    advanced = shifted(partial_sums + reflect[None, :] * term, "col", 1)
    return advanced


def solution(mesh):
    placed = (
        P(None, "row"),
        P(None, "row"),
        P("row"),
        P(None, "row"),
        P("row"),
        P("col", "row"),
        P("row", None),
        P(),
    )
    return jax.shard_map(
        on_device, mesh=mesh, in_specs=placed, out_specs=P("col", "row"), check_vma=False
    )
```

profile of v0, /device:TPU:0, one launch (start us, length us, event | category | flops | bytes accessed | tf_op | source)
XLA Modules:
  0.0 541.3 jit_solution(14267143060094143835)
XLA Ops:
  12.6 53.0 %all-reduce.6.cloned.1.call-done = (bf16[3,6144]{1,0:T(4,128)(2,1)}, bf16[3,6144]{1,0:T(4,128)(2,1)}, bf16[6144]{0:T(1024)(128)(2,1)}) async-done(((bf16[3,6144]{1,0:T(4,128)(2,1)}, bf16[3,6144]{1,0:T(4,128)(2,1)}, bf16[6144]{0:T(1024)(128)(2,1)}), (bf16[3,6144]{1,0:T(4,128)(2,1)}, bf16[3,6144]{1,0:T(4,128)(2,1)}, bf16[6144]{0:T(1024)(128)(2,1)})) %all-reduce.6.cloned.1.call-update) | async-done | bytes 86032 | tf_op jit(solution)/shard_map/psum | solution.py:11
  65.7 58.3 %all-reduce.4.cloned.1.call-done = bf16[32,6144]{1,0:T(8,128)(2,1)} async-done(((bf16[32,6144]{1,0:T(8,128)(2,1)}), bf16[32,6144]{1,0:T(8,128)(2,1)}) %all-reduce.4.cloned.1.call-update) | async-done | bytes 393232 | tf_op jit(solution)/shard_map/psum | solution.py:11
  124.5 387.6 %while.22 = (s32[]{:T(128)}, f32[6,32,1024]{2,1,0:T(8,128)}, s32[6]{0:T(128)}, s32[48,48]{1,0:T(8,128)}, bf16[3,6144]{1,0:T(4,128)(2,1)}, /*index=5*/bf16[3,6144...) while((s32[]{:T(128)}, f32[6,32,1024]{2,1,0:T(8,128)}, ...), condition=%wide.region_7.8_spmd, body=%wide.region_4.7_spmd.sunk | while | flops 197218464 | bytes 17790688 | solution.py:92
  128.4 60.0 %while.23 = (s32[]{:T(128)}, f32[32,1024]{1,0:T(8,128)S(1)}, s32[3]{0:T(128)S(1)}, bf16[32,6144]{1,0:T(8,128)(2,1)}, bf16[3,6144]{1,0:T(4,128)(2,1)}, /*index=5*...) while((s32[]{:T(128)}, f32[32,1024]{1,0:T(8,128)S(1)}, ...), condition=%wide.region_6.6_spmd.clone, body=%wide.region_5.5_spmd.clone.sunk | while | flops 197212304 | bytes 17487640 | solution.py:89
  131.9 3.8 broadcast_in_dim.30
  135.8 12.7 %fusion.42 = f32[32,1024]{1,0:T(8,128)S(1)} fusion(f32[128,8,16,128]{3,2,1,0:T(8,128)} %bitcast.70, f32[2048]{0:T(1024)S(1)} %dynamic-slice_convert_fusion.12, f32[1024]{0:T(1024)S(1)} %bitcast.82, f32[1024]{0:T(1024)S(1)} %bitcast.81, f32[1024]{0:T(1024)S(1)} %bitcast.83, f32[2048]{0:T(1024)S(1)} %bitcast.72, f32[1024]{0:T(1024)S(1)} %bitcast.79, ...), kind=kOutput, calls=%fused_computation.28.clone.1 | convolution fusion | flops 197197824 | bytes 8863749 | tf_op jit(solution)/shard_map/while/body/eval_jaxpr/while/body/eval_jaxpr/dot_general | solution.py:86
  151.9 3.8 broadcast_in_dim.30
  155.8 12.7 %fusion.42 = f32[32,1024]{1,0:T(8,128)S(1)} fusion(f32[128,8,16,128]{3,2,1,0:T(8,128)} %bitcast.70, f32[2048]{0:T(1024)S(1)} %dynamic-slice_convert_fusion.12, f32[1024]{0:T(1024)S(1)} %bitcast.82, f32[1024]{0:T(1024)S(1)} %bitcast.81, f32[1024]{0:T(1024)S(1)} %bitcast.83, f32[2048]{0:T(1024)S(1)} %bitcast.72, f32[1024]{0:T(1024)S(1)} %bitcast.79, ...), kind=kOutput, calls=%fused_computation.28.clone.1 | convolution fusion | flops 197197824 | bytes 8863749 | tf_op jit(solution)/shard_map/while/body/eval_jaxpr/while/body/eval_jaxpr/dot_general | solution.py:86
  171.9 3.8 broadcast_in_dim.30
  175.8 12.7 %fusion.42 = f32[32,1024]{1,0:T(8,128)S(1)} fusion(f32[128,8,16,128]{3,2,1,0:T(8,128)} %bitcast.70, f32[2048]{0:T(1024)S(1)} %dynamic-slice_convert_fusion.12, f32[1024]{0:T(1024)S(1)} %bitcast.82, f32[1024]{0:T(1024)S(1)} %bitcast.81, f32[1024]{0:T(1024)S(1)} %bitcast.83, f32[2048]{0:T(1024)S(1)} %bitcast.72, f32[1024]{0:T(1024)S(1)} %bitcast.79, ...), kind=kOutput, calls=%fused_computation.28.clone.1 | convolution fusion | flops 197197824 | bytes 8863749 | tf_op jit(solution)/shard_map/while/body/eval_jaxpr/while/body/eval_jaxpr/dot_general | solution.py:86
  193.0 60.0 %while.23 = (s32[]{:T(128)}, f32[32,1024]{1,0:T(8,128)S(1)}, s32[3]{0:T(128)S(1)}, bf16[32,6144]{1,0:T(8,128)(2,1)}, bf16[3,6144]{1,0:T(4,128)(2,1)}, /*index=5*...) while((s32[]{:T(128)}, f32[32,1024]{1,0:T(8,128)S(1)}, ...), condition=%wide.region_6.6_spmd.clone, body=%wide.region_5.5_spmd.clone.sunk | while | flops 197212304 | bytes 17487640 | solution.py:89
  196.5 3.8 broadcast_in_dim.30
  200.3 12.7 %fusion.42 = f32[32,1024]{1,0:T(8,128)S(1)} fusion(f32[128,8,16,128]{3,2,1,0:T(8,128)} %bitcast.70, f32[2048]{0:T(1024)S(1)} %dynamic-slice_convert_fusion.12, f32[1024]{0:T(1024)S(1)} %bitcast.82, f32[1024]{0:T(1024)S(1)} %bitcast.81, f32[1024]{0:T(1024)S(1)} %bitcast.83, f32[2048]{0:T(1024)S(1)} %bitcast.72, f32[1024]{0:T(1024)S(1)} %bitcast.79, ...), kind=kOutput, calls=%fused_computation.28.clone.1 | convolution fusion | flops 197197824 | bytes 8863749 | tf_op jit(solution)/shard_map/while/body/eval_jaxpr/while/body/eval_jaxpr/dot_general | solution.py:86
  220.4 12.7 %fusion.42 = f32[32,1024]{1,0:T(8,128)S(1)} fusion(f32[128,8,16,128]{3,2,1,0:T(8,128)} %bitcast.70, f32[2048]{0:T(1024)S(1)} %dynamic-slice_convert_fusion.12, f32[1024]{0:T(1024)S(1)} %bitcast.82, f32[1024]{0:T(1024)S(1)} %bitcast.81, f32[1024]{0:T(1024)S(1)} %bitcast.83, f32[2048]{0:T(1024)S(1)} %bitcast.72, f32[1024]{0:T(1024)S(1)} %bitcast.79, ...), kind=kOutput, calls=%fused_computation.28.clone.1 | convolution fusion | flops 197197824 | bytes 8863749 | tf_op jit(solution)/shard_map/while/body/eval_jaxpr/while/body/eval_jaxpr/dot_general | solution.py:86
  240.4 12.7 %fusion.42 = f32[32,1024]{1,0:T(8,128)S(1)} fusion(f32[128,8,16,128]{3,2,1,0:T(8,128)} %bitcast.70, f32[2048]{0:T(1024)S(1)} %dynamic-slice_convert_fusion.12, f32[1024]{0:T(1024)S(1)} %bitcast.82, f32[1024]{0:T(1024)S(1)} %bitcast.81, f32[1024]{0:T(1024)S(1)} %bitcast.83, f32[2048]{0:T(1024)S(1)} %bitcast.72, f32[1024]{0:T(1024)S(1)} %bitcast.79, ...), kind=kOutput, calls=%fused_computation.28.clone.1 | convolution fusion | flops 197197824 | bytes 8863749 | tf_op jit(solution)/shard_map/while/body/eval_jaxpr/while/body/eval_jaxpr/dot_general | solution.py:86
  257.6 60.0 %while.23 = (s32[]{:T(128)}, f32[32,1024]{1,0:T(8,128)S(1)}, s32[3]{0:T(128)S(1)}, bf16[32,6144]{1,0:T(8,128)(2,1)}, bf16[3,6144]{1,0:T(4,128)(2,1)}, /*index=5*...) while((s32[]{:T(128)}, f32[32,1024]{1,0:T(8,128)S(1)}, ...), condition=%wide.region_6.6_spmd.clone, body=%wide.region_5.5_spmd.clone.sunk | while | flops 197212304 | bytes 17487640 | solution.py:89
  264.9 12.7 %fusion.42 = f32[32,1024]{1,0:T(8,128)S(1)} fusion(f32[128,8,16,128]{3,2,1,0:T(8,128)} %bitcast.70, f32[2048]{0:T(1024)S(1)} %dynamic-slice_convert_fusion.12, f32[1024]{0:T(1024)S(1)} %bitcast.82, f32[1024]{0:T(1024)S(1)} %bitcast.81, f32[1024]{0:T(1024)S(1)} %bitcast.83, f32[2048]{0:T(1024)S(1)} %bitcast.72, f32[1024]{0:T(1024)S(1)} %bitcast.79, ...), kind=kOutput, calls=%fused_computation.28.clone.1 | convolution fusion | flops 197197824 | bytes 8863749 | tf_op jit(solution)/shard_map/while/body/eval_jaxpr/while/body/eval_jaxpr/dot_general | solution.py:86
  284.9 12.7 %fusion.42 = f32[32,1024]{1,0:T(8,128)S(1)} fusion(f32[128,8,16,128]{3,2,1,0:T(8,128)} %bitcast.70, f32[2048]{0:T(1024)S(1)} %dynamic-slice_convert_fusion.12, f32[1024]{0:T(1024)S(1)} %bitcast.82, f32[1024]{0:T(1024)S(1)} %bitcast.81, f32[1024]{0:T(1024)S(1)} %bitcast.83, f32[2048]{0:T(1024)S(1)} %bitcast.72, f32[1024]{0:T(1024)S(1)} %bitcast.79, ...), kind=kOutput, calls=%fused_computation.28.clone.1 | convolution fusion | flops 197197824 | bytes 8863749 | tf_op jit(solution)/shard_map/while/body/eval_jaxpr/while/body/eval_jaxpr/dot_general | solution.py:86
  304.9 12.7 %fusion.42 = f32[32,1024]{1,0:T(8,128)S(1)} fusion(f32[128,8,16,128]{3,2,1,0:T(8,128)} %bitcast.70, f32[2048]{0:T(1024)S(1)} %dynamic-slice_convert_fusion.12, f32[1024]{0:T(1024)S(1)} %bitcast.82, f32[1024]{0:T(1024)S(1)} %bitcast.81, f32[1024]{0:T(1024)S(1)} %bitcast.83, f32[2048]{0:T(1024)S(1)} %bitcast.72, f32[1024]{0:T(1024)S(1)} %bitcast.79, ...), kind=kOutput, calls=%fused_computation.28.clone.1 | convolution fusion | flops 197197824 | bytes 8863749 | tf_op jit(solution)/shard_map/while/body/eval_jaxpr/while/body/eval_jaxpr/dot_general | solution.py:86
  322.2 60.0 %while.23 = (s32[]{:T(128)}, f32[32,1024]{1,0:T(8,128)S(1)}, s32[3]{0:T(128)S(1)}, bf16[32,6144]{1,0:T(8,128)(2,1)}, bf16[3,6144]{1,0:T(4,128)(2,1)}, /*index=5*...) while((s32[]{:T(128)}, f32[32,1024]{1,0:T(8,128)S(1)}, ...), condition=%wide.region_6.6_spmd.clone, body=%wide.region_5.5_spmd.clone.sunk | while | flops 197212304 | bytes 17487640 | solution.py:89
  329.5 12.7 %fusion.42 = f32[32,1024]{1,0:T(8,128)S(1)} fusion(f32[128,8,16,128]{3,2,1,0:T(8,128)} %bitcast.70, f32[2048]{0:T(1024)S(1)} %dynamic-slice_convert_fusion.12, f32[1024]{0:T(1024)S(1)} %bitcast.82, f32[1024]{0:T(1024)S(1)} %bitcast.81, f32[1024]{0:T(1024)S(1)} %bitcast.83, f32[2048]{0:T(1024)S(1)} %bitcast.72, f32[1024]{0:T(1024)S(1)} %bitcast.79, ...), kind=kOutput, calls=%fused_computation.28.clone.1 | convolution fusion | flops 197197824 | bytes 8863749 | tf_op jit(solution)/shard_map/while/body/eval_jaxpr/while/body/eval_jaxpr/dot_general | solution.py:86
  349.5 12.7 %fusion.42 = f32[32,1024]{1,0:T(8,128)S(1)} fusion(f32[128,8,16,128]{3,2,1,0:T(8,128)} %bitcast.70, f32[2048]{0:T(1024)S(1)} %dynamic-slice_convert_fusion.12, f32[1024]{0:T(1024)S(1)} %bitcast.82, f32[1024]{0:T(1024)S(1)} %bitcast.81, f32[1024]{0:T(1024)S(1)} %bitcast.83, f32[2048]{0:T(1024)S(1)} %bitcast.72, f32[1024]{0:T(1024)S(1)} %bitcast.79, ...), kind=kOutput, calls=%fused_computation.28.clone.1 | convolution fusion | flops 197197824 | bytes 8863749 | tf_op jit(solution)/shard_map/while/body/eval_jaxpr/while/body/eval_jaxpr/dot_general | solution.py:86
  369.5 12.7 %fusion.42 = f32[32,1024]{1,0:T(8,128)S(1)} fusion(f32[128,8,16,128]{3,2,1,0:T(8,128)} %bitcast.70, f32[2048]{0:T(1024)S(1)} %dynamic-slice_convert_fusion.12, f32[1024]{0:T(1024)S(1)} %bitcast.82, f32[1024]{0:T(1024)S(1)} %bitcast.81, f32[1024]{0:T(1024)S(1)} %bitcast.83, f32[2048]{0:T(1024)S(1)} %bitcast.72, f32[1024]{0:T(1024)S(1)} %bitcast.79, ...), kind=kOutput, calls=%fused_computation.28.clone.1 | convolution fusion | flops 197197824 | bytes 8863749 | tf_op jit(solution)/shard_map/while/body/eval_jaxpr/while/body/eval_jaxpr/dot_general | solution.py:86
  386.8 60.0 %while.23 = (s32[]{:T(128)}, f32[32,1024]{1,0:T(8,128)S(1)}, s32[3]{0:T(128)S(1)}, bf16[32,6144]{1,0:T(8,128)(2,1)}, bf16[3,6144]{1,0:T(4,128)(2,1)}, /*index=5*...) while((s32[]{:T(128)}, f32[32,1024]{1,0:T(8,128)S(1)}, ...), condition=%wide.region_6.6_spmd.clone, body=%wide.region_5.5_spmd.clone.sunk | while | flops 197212304 | bytes 17487640 | solution.py:89
  394.1 12.7 %fusion.42 = f32[32,1024]{1,0:T(8,128)S(1)} fusion(f32[128,8,16,128]{3,2,1,0:T(8,128)} %bitcast.70, f32[2048]{0:T(1024)S(1)} %dynamic-slice_convert_fusion.12, f32[1024]{0:T(1024)S(1)} %bitcast.82, f32[1024]{0:T(1024)S(1)} %bitcast.81, f32[1024]{0:T(1024)S(1)} %bitcast.83, f32[2048]{0:T(1024)S(1)} %bitcast.72, f32[1024]{0:T(1024)S(1)} %bitcast.79, ...), kind=kOutput, calls=%fused_computation.28.clone.1 | convolution fusion | flops 197197824 | bytes 8863749 | tf_op jit(solution)/shard_map/while/body/eval_jaxpr/while/body/eval_jaxpr/dot_general | solution.py:86
  414.1 12.7 %fusion.42 = f32[32,1024]{1,0:T(8,128)S(1)} fusion(f32[128,8,16,128]{3,2,1,0:T(8,128)} %bitcast.70, f32[2048]{0:T(1024)S(1)} %dynamic-slice_convert_fusion.12, f32[1024]{0:T(1024)S(1)} %bitcast.82, f32[1024]{0:T(1024)S(1)} %bitcast.81, f32[1024]{0:T(1024)S(1)} %bitcast.83, f32[2048]{0:T(1024)S(1)} %bitcast.72, f32[1024]{0:T(1024)S(1)} %bitcast.79, ...), kind=kOutput, calls=%fused_computation.28.clone.1 | convolution fusion | flops 197197824 | bytes 8863749 | tf_op jit(solution)/shard_map/while/body/eval_jaxpr/while/body/eval_jaxpr/dot_general | solution.py:86
  434.1 12.7 %fusion.42 = f32[32,1024]{1,0:T(8,128)S(1)} fusion(f32[128,8,16,128]{3,2,1,0:T(8,128)} %bitcast.70, f32[2048]{0:T(1024)S(1)} %dynamic-slice_convert_fusion.12, f32[1024]{0:T(1024)S(1)} %bitcast.82, f32[1024]{0:T(1024)S(1)} %bitcast.81, f32[1024]{0:T(1024)S(1)} %bitcast.83, f32[2048]{0:T(1024)S(1)} %bitcast.72, f32[1024]{0:T(1024)S(1)} %bitcast.79, ...), kind=kOutput, calls=%fused_computation.28.clone.1 | convolution fusion | flops 197197824 | bytes 8863749 | tf_op jit(solution)/shard_map/while/body/eval_jaxpr/while/body/eval_jaxpr/dot_general | solution.py:86
  451.4 60.0 %while.23 = (s32[]{:T(128)}, f32[32,1024]{1,0:T(8,128)S(1)}, s32[3]{0:T(128)S(1)}, bf16[32,6144]{1,0:T(8,128)(2,1)}, bf16[3,6144]{1,0:T(4,128)(2,1)}, /*index=5*...) while((s32[]{:T(128)}, f32[32,1024]{1,0:T(8,128)S(1)}, ...), condition=%wide.region_6.6_spmd.clone, body=%wide.region_5.5_spmd.clone.sunk | while | flops 197212304 | bytes 17487640 | solution.py:89
  458.7 12.7 %fusion.42 = f32[32,1024]{1,0:T(8,128)S(1)} fusion(f32[128,8,16,128]{3,2,1,0:T(8,128)} %bitcast.70, f32[2048]{0:T(1024)S(1)} %dynamic-slice_convert_fusion.12, f32[1024]{0:T(1024)S(1)} %bitcast.82, f32[1024]{0:T(1024)S(1)} %bitcast.81, f32[1024]{0:T(1024)S(1)} %bitcast.83, f32[2048]{0:T(1024)S(1)} %bitcast.72, f32[1024]{0:T(1024)S(1)} %bitcast.79, ...), kind=kOutput, calls=%fused_computation.28.clone.1 | convolution fusion | flops 197197824 | bytes 8863749 | tf_op jit(solution)/shard_map/while/body/eval_jaxpr/while/body/eval_jaxpr/dot_general | solution.py:86
  478.7 12.7 %fusion.42 = f32[32,1024]{1,0:T(8,128)S(1)} fusion(f32[128,8,16,128]{3,2,1,0:T(8,128)} %bitcast.70, f32[2048]{0:T(1024)S(1)} %dynamic-slice_convert_fusion.12, f32[1024]{0:T(1024)S(1)} %bitcast.82, f32[1024]{0:T(1024)S(1)} %bitcast.81, f32[1024]{0:T(1024)S(1)} %bitcast.83, f32[2048]{0:T(1024)S(1)} %bitcast.72, f32[1024]{0:T(1024)S(1)} %bitcast.79, ...), kind=kOutput, calls=%fused_computation.28.clone.1 | convolution fusion | flops 197197824 | bytes 8863749 | tf_op jit(solution)/shard_map/while/body/eval_jaxpr/while/body/eval_jaxpr/dot_general | solution.py:86
  498.7 12.7 %fusion.42 = f32[32,1024]{1,0:T(8,128)S(1)} fusion(f32[128,8,16,128]{3,2,1,0:T(8,128)} %bitcast.70, f32[2048]{0:T(1024)S(1)} %dynamic-slice_convert_fusion.12, f32[1024]{0:T(1024)S(1)} %bitcast.82, f32[1024]{0:T(1024)S(1)} %bitcast.81, f32[1024]{0:T(1024)S(1)} %bitcast.83, f32[2048]{0:T(1024)S(1)} %bitcast.72, f32[1024]{0:T(1024)S(1)} %bitcast.79, ...), kind=kOutput, calls=%fused_computation.28.clone.1 | convolution fusion | flops 197197824 | bytes 8863749 | tf_op jit(solution)/shard_map/while/body/eval_jaxpr/while/body/eval_jaxpr/dot_general | solution.py:86
  514.8 18.7 %collective-permute-done = f32[32,6144]{1,0:T(8,128)S(1)} collective-permute-done((f32[32,6144]{1,0:T(8,128)S(1)}, f32[32,6144]{1,0:T(8,128)S(1)}, u32[]{:S(2)}, u32[]{:S(2)}) %collective-permute-start) | collective-permute-done | bytes 786464 | tf_op jit(solution)/shard_map/ppermute | solution.py:17
  (196 shorter events, 122.4 us)
Async XLA Ops:
  6.5 5.4 %copy-start = (s32[48,384]{1,0:T(8,128)S(1)}, s32[48,384]{1,0:T(8,128)}, u32[]{:S(2)}) copy-start(s32[48,384]{1,0:T(8,128)} %param.18) | copy-start | bytes 221188
  6.5 59.2 %all-reduce.6.cloned.1.call-start = ((), (), s32[]{:S(2)}) async-start(), calls=%async_computation.1 | async-start | bytes 221184 | tf_op jit(solution)/shard_map/psum | solution.py:11
  10.1 113.9 %all-reduce.4.cloned.1.call-start = ((), (), s32[]{:S(2)}) async-start(), calls=%async_computation | async-start | bytes 786432 | tf_op jit(solution)/shard_map/psum | solution.py:11
  124.5 388.8 %copy-start.1 = (f32[32,6144]{1,0:T(8,128)S(1)}, f32[32,6144]{1,0:T(8,128)}, u32[]{:S(2)}) copy-start(f32[32,6144]{1,0:T(8,128)} %param.17) | copy-start | bytes 2359300
  124.5 388.8 %copy-start.2 = (f32[6144]{0:T(1024)S(1)}, f32[6144]{0:T(1024)}, u32[]{:S(2)}) copy-start(f32[6144]{0:T(1024)} %param.16) | copy-start | bytes 73732
  513.4 20.2 %collective-permute-start = (f32[32,6144]{1,0:T(8,128)S(1)}, f32[32,6144]{1,0:T(8,128)S(1)}, u32[]{:S(2)}, u32[]{:S(2)}) collective-permute-start(f32[32,6144]{1,0:T(8,128)S(1)} %multiply_add_fusion), channel_id=1, source_target_pairs={{3,0},{0,1},{1,2},{2,3},{7,4},{4,5},{5,6},{6,7},{11,8},{8,9},{9,10... | collective-permute-start | bytes 2359304 | tf_op jit(solution)/shard_map/ppermute | solution.py:17
Sparse Core Ops, SparseCore 0:
  10.7 54.9 all-reduce.5
  69.1 54.8 all-reduce.3
where the time goes:
time: 547 us; the launch traced here: 541 us
  matrix products  228 us (42%)
  waiting for transfers between devices  130 us (24%)
  local copies, waits for them, and re-layouts  99.9 us (18%)
  other arithmetic  36.2 us (7%)
  loops' own time  31.5 us (6%)
  between operations  14.2 us (3%)
    dot_general x18, matrix products, one_column(): jnp.dot(erad, view.T, preferred_element_type=jnp.float32)  228 us
    psum x2, waiting for transfers between devices, from_root(): return lax.psum(jnp.where(mine, shard, jnp.zeros_like(shard)), axis)  111 us
    broadcast_in_dim x18, local copies, waits for them, and re-layouts, one_column(): jnp.broadcast_to(matrix_tile_block[:, None, :, None], (receiver_tile_coun...  69 us
    another operation x6, loops' own time, one_block(): lax.scan(one_column, init, jnp.arange(ccount, dtype=jnp.int32))  23.7 us
    ppermute x1, waiting for transfers between devices, shifted(): return lax.ppermute(block, axis, route)  18.7 us
    convert_element_type x18, other arithmetic, one_column(): lax.dynamic_slice_in_dim(em_pos, cstart, column_block_size, 1)  13.4 us
    convert_element_type x18, other arithmetic, one_column(): lax.dynamic_slice_in_dim(em_area, cstart, column_block_size, 0)  12.4 us
    dynamic_slice x18, local copies, waits for them, and re-layouts, one_block(): lax.scan(one_column, init, jnp.arange(ccount, dtype=jnp.int32))  11.2 us
  transfers between devices with their start and end apart: 3, of which 3 were waited for; matrix products, arithmetic and copies ran while one was open for 0% of the time, Pallas kernels for 0%

commit v1 on v0

v1 whole, which is shorter than its diff:
```python
import functools
import math

import jax
import jax.numpy as jnp
from jax import lax
from jax.experimental import pallas as pl
from jax.experimental.pallas import tpu as pltpu
from jax.sharding import PartitionSpec as P

BF = jnp.bfloat16
F32 = jnp.float32
TILE = 128
FEATURES = 32
BITS = 6
GROUP = 4
STEP = 4
MATMUL_COS = 2
KAPPA = (math.pi - 1) / (2 * math.pi)
SIGMA = (math.pi + 1) / (2 * math.pi)


def split3(x):
    high = lax.reduce_precision(x, 8, 7)
    rest = x - high
    mid = lax.reduce_precision(rest, 8, 7)
    return high.astype(BF), mid.astype(BF), (rest - mid).astype(BF)


def filled(rows):
    return rows + [jnp.zeros_like(rows[0])] * (FEATURES - len(rows))


def receiver_features(pos, nrm):
    p, n = pos.astype(F32), nrm.astype(F32)
    square = split3(p[0] * p[0] + p[1] * p[1] + p[2] * p[2])
    own = split3(-(n[0] * p[0] + n[1] * p[1] + n[2] * p[2]))
    one = jnp.ones_like(pos[0])
    rows = [pos[i] for i in range(3) for _ in range(3)]
    rows += [square[i] for i in (0, 0, 1, 1, 0, 2)] + [one] * 3
    rows += [nrm[0], nrm[1], nrm[2], *own]
    return jnp.stack(filled(rows), 0).reshape(FEATURES, -1, TILE).transpose(1, 2, 0)


def emitter_features(pos, nrm, area):
    p, n, a = pos.astype(F32), nrm.astype(F32), area.astype(F32)
    scale = 1.0 / (KAPPA * a)
    gain = 1.0 / (math.pi * KAPPA * KAPPA * a)
    one, zero = jnp.ones_like(pos[0]), jnp.zeros_like(pos[0])
    s = split3(scale)
    t = split3(scale * (p[0] * p[0] + p[1] * p[1] + p[2] * p[2]) + SIGMA / KAPPA)
    e = [gain * n[0], gain * n[1], gain * n[2]]
    e.append(-(e[0] * p[0] + e[1] * p[1] + e[2] * p[2]))
    width = [x for i in range(3) for x in split3(-2.0 * scale * p[i])]
    width += [s[i] for i in (0, 1, 0, 1, 2, 0)] + list(t)
    receive = [zero] * 18 + [pos[0], pos[1], pos[2], one, one, one]
    emit = [x for i in range(3) for x in split3(e[i])] + [zero] * 6 + list(split3(e[3]))
    f = jnp.stack([jnp.stack(filled(r), 0) for r in (width, receive, emit)], 0)
    f = f.reshape(3, FEATURES, -1, TILE).transpose(2, 1, 0, 3)
    f = f.reshape(-1, FEATURES, 3 * TILE)
    f = jnp.concatenate([f, jnp.zeros_like(f[:1])], 0)
    e = jnp.stack(e + [jnp.zeros_like(e[0])] * 4, 0).reshape(8, -1, TILE).transpose(1, 0, 2)
    return f, jnp.concatenate([e, jnp.zeros_like(e[:1])], 0)


def visible_groups(mask):
    n_rec, n_em = mask.shape
    cum = jnp.cumsum(mask, axis=1)
    groups = (cum[:, -1] + GROUP - 1) // GROUP
    ends = jnp.cumsum(groups)
    length = n_rec * ((n_em + GROUP - 1) // GROUP) + 2 * STEP
    q = jnp.arange(length, dtype=jnp.int32)
    a = jnp.sum((ends[None, :] <= q[:, None]).astype(jnp.int32), axis=1)
    hot = a[:, None] == jnp.arange(n_rec, dtype=jnp.int32)[None, :]
    rows = jnp.dot(hot.astype(F32), cum.astype(F32), preferred_element_type=F32)
    first = jnp.sum(jnp.where(hot, (ends - groups)[None, :], 0), axis=1)
    rank = (GROUP * (q - first)).astype(F32)
    code = jnp.minimum(a, n_rec - 1)
    for t in range(GROUP):
        code = (code << BITS) + jnp.sum((rows <= rank[:, None] + t).astype(jnp.int32), axis=1)
    return ends[-1:], code


def decoded(code):
    last = (1 << BITS) - 1
    return code >> (BITS * GROUP), [
        (code >> (BITS * (GROUP - 1 - t))) & last for t in range(GROUP)
    ]


def term_kernel(count, codes, rec, em, emit_rows, rad, out, place, view):
    steps = (count[0] + STEP - 1) // STEP
    out[...] = jnp.zeros_like(out)
    view[...] = jnp.zeros_like(view)

    row = lax.broadcasted_iota(jnp.int32, (FEATURES, 3 * TILE), 0)
    col = lax.broadcasted_iota(jnp.int32, (FEATURES, 3 * TILE), 1)
    chosen = jnp.where(row == 3 * (col // TILE), 1.0, 0.0).astype(BF)

    def spread(a, carry):
        spreaded = jnp.dot(rec[a], chosen, preferred_element_type=F32)
        for i in range(3):
            place[a, i] = spreaded[:, i * TILE : (i + 1) * TILE]
        return carry

    lax.fori_loop(0, rec.shape[0], spread, 0, unroll=4)

    def views(a, tiles, slot):
        products = [
            jnp.dot(
                rec[a],
                em[b] if t < MATMUL_COS else em[b, :, : 2 * TILE],
                preferred_element_type=F32,
            )
            for t, b in enumerate(tiles)
        ]
        for r in range(0, TILE, 32):
            x, y, z = (place[a, i, r : r + 32] for i in range(3))
            for t, b in enumerate(tiles):
                m = products[t][r : r + 32]
                if t < MATMUL_COS:
                    cos = m[:, 2 * TILE :]
                else:
                    e = [emit_rows[b, i : i + 1] for i in range(4)]
                    cos = e[0] * x + e[1] * y + e[2] * z + e[3]
                w = m[:, :TILE]
                v = jnp.maximum(cos, 0.0) * m[:, TILE : 2 * TILE]
                v = v * pltpu.reciprocal(w * w - 1.0, approx=True)
                view[slot, r : r + 32, t * TILE : (t + 1) * TILE] = jnp.maximum(v.astype(BF), 0)

    def add(a, tiles, slot):
        r = jnp.concatenate([rad[b] for b in tiles], axis=1)
        at = pl.ds(pl.multiple_of(a * TILE, TILE), TILE)
        out[:, at] += lax.dot_general(
            r, view[slot], (((1,), (1,)), ((), ())), preferred_element_type=F32
        )

    def step(i, carry):
        for j in range(STEP):
            add(*decoded(codes[jnp.maximum(i - 1, 0) * STEP + j]), j)
            views(*decoded(codes[i * STEP + j]), j)
        return carry

    lax.fori_loop(0, steps + 1, step, 0)


def block_term(count, codes, rec, em, emit_rows, rad):
    tiles, cases = rec.shape[0], rad.shape[1]
    smem = pl.BlockSpec(memory_space=pltpu.SMEM)
    vmem = pl.BlockSpec(memory_space=pltpu.VMEM)
    pairs = tiles * tiles * TILE * TILE
    return pl.pallas_call(
        term_kernel,
        out_shape=jax.ShapeDtypeStruct((cases, tiles * TILE), F32),
        in_specs=[smem] * 2 + [vmem] * 4,
        out_specs=vmem,
        scratch_shapes=[
            pltpu.VMEM((tiles, 3, TILE, TILE), F32),
            pltpu.VMEM((STEP, TILE, GROUP * TILE), BF),
        ],
        compiler_params=pltpu.CompilerParams(vmem_limit_bytes=56 * 2**20),
        cost_estimate=pl.CostEstimate(
            flops=pairs * 200, bytes_accessed=8 * 2**20, transcendentals=pairs
        ),
        name="block_term",
    )(count, codes, rec, em, emit_rows, rad)


def from_root(block, axis, root):
    n = lax.axis_size(axis)
    me = lax.axis_index(axis)
    bit = 1
    while bit < n:
        got = lax.ppermute(block, axis, [(i, i ^ bit) for i in range(n)])
        block = jnp.where((me & bit) == (root & bit), block, got)
        bit *= 2
    return block


def shifted(block, axis, distance):
    n = lax.axis_size(axis)
    return lax.ppermute(block, axis, [((i - distance) % n, i) for i in range(n)])


def on_device(positions, normals, areas, radiosity, reflect, partial_sums, visible, section):
    carried = shifted(partial_sums, "col", 1)
    n_row = lax.axis_size("row")
    emit = (lax.axis_index("col") + section[0]) % n_row
    tiles = positions.shape[1] // TILE
    packed = jnp.concatenate([positions, normals, areas[None], radiosity], 0)
    packed = from_root(packed, "row", emit)
    mask = lax.dynamic_slice_in_dim(visible, emit * tiles, tiles, 1)
    count, codes = visible_groups(mask)
    rec = receiver_features(positions, normals)
    em, emit_rows = emitter_features(packed[:3], packed[3:6], packed[6])
    rad = packed[7:]
    rad = rad.reshape(rad.shape[0], -1, TILE).transpose(1, 0, 2)
    rad = jnp.concatenate([rad, jnp.zeros_like(rad[:1])], 0)
    term = block_term(count, codes, rec, em, emit_rows, rad)
    return carried + reflect[None, :] * term


def solution(mesh):
    placed = (
        P(None, "row"),
        P(None, "row"),
        P("row"),
        P(None, "row"),
        P("row"),
        P("col", "row"),
        P("row", None),
        P(),
    )
    return jax.shard_map(
        on_device, mesh=mesh, in_specs=placed, out_specs=P("col", "row"), check_vma=False
    )
```

time: 547 us -> 118 us (0.22)
  matrix products: 228 us -> 0.26 us
  waiting for transfers between devices: 130 us -> 19.6 us
  local copies, waits for them, and re-layouts: 99.9 us -> 11.6 us
  Pallas kernels: 0 us -> 71 us
  loops' own time: 31.5 us -> 0 us
  other arithmetic: 36.2 us -> 6.95 us
  between operations: 14.2 us -> 1.12 us
    dot_general x18 -> x1, matrix products: 228 us -> 0.26 us  [visible_groups(): rows = jnp.dot(hot.astype(F32), cum.astype(F32), preferred_element_type=F32)]
    psum x2 -> x0, waiting for transfers between devices: 111 us -> none  [from_root(): return lax.psum(jnp.where(mine, shard, jnp.zeros_like(shard)), axis)]
    pallas_call x0 -> x1, Pallas kernels: none -> 71 us  [block_term(): pl.pallas_call(term_kernel, out_shape=jax.ShapeDtypeStruct((cases, tiles...]
    broadcast_in_dim x18 -> x1, local copies, waits for them, and re-layouts: 69 us -> 0.75 us  [on_device(): packed = jnp.concatenate([positions, normals, areas[None], radiosity], 0)]
    another operation x7 -> x0, loops' own time: 31.5 us -> none  [the longest x6 23.7 us: one_block(): lax.scan(one_column, init, jnp.arange(ccount, dtype=jnp.int32))]
    convert_element_type x60 -> x13, other arithmetic: 31.5 us -> 1.21 us  [the longest x10 1.18 us: split3(): return (high.astype(BF), mid.astype(BF), (rest - mid).astype(BF))]
    dynamic_slice x31 -> x1, local copies, waits for them, and re-layouts: 23.3 us -> 0.08 us  [on_device(): mask = lax.dynamic_slice_in_dim(visible, emit * tiles, tiles, 1)]
    ppermute x1 -> x4, waiting for transfers between devices: 18.7 us -> 19.6 us  [the longest x3 19.6 us: from_root(): got = lax.ppermute(block, axis, [(i, i ^ bit) for i in range(n)])]
  transfers between devices with their start and end apart: 3 -> 4, of which waited for: 3 -> 2; matrix products, arithmetic and copies ran while one was open for 0% -> 12% of each run, Pallas kernels for 0% -> 61%
where the time goes in v1:
time: 118 us; the launch traced here: 117 us
  Pallas kernels  71 us (60%)
  waiting for transfers between devices  19.6 us (17%)
  local copies, waits for them, and re-layouts  11.6 us (10%)
  other arithmetic  6.95 us (6%)
  starting transfers between devices  6.3 us (5%)
    pallas_call x1, Pallas kernels, block_term(): pl.pallas_call(term_kernel, out_shape=jax.ShapeDtypeStruct((cases, tiles...  71 us
    ppermute x3, waiting for transfers between devices, from_root(): got = lax.ppermute(block, axis, [(i, i ^ bit) for i in range(n)])  19.6 us
    ppermute x3, starting transfers between devices, from_root(): got = lax.ppermute(block, axis, [(i, i ^ bit) for i in range(n)])  3.67 us
    ppermute x1, starting transfers between devices, shifted(): lax.ppermute(block, axis, [((i - distance) % n, i) for i in range(n)])  2.64 us
  transfers between devices with their start and end apart: 4, of which 2 were waited for; matrix products, arithmetic and copies ran while one was open for 12% of the time, Pallas kernels for 61%

profile of v1, /device:TPU:0, one launch (start us, length us, event | category | flops | bytes accessed | tf_op | source)
XLA Modules:
  0.0 116.9 jit_solution(11513897149367675594)
XLA Ops:
  0.0 0.8 broadcast_in_dim.12
  0.8 1.3 %pad_maximum_fusion = bf16[39,6144]{1,0:T(8,128)(2,1)S(1)} fusion(bf16[32,6144]{1,0:T(8,128)(2,1)} %param.11, bf16[1,6144]{1,0:T(2,128)(2,1)S(1)} %broadcast_in_dim.12, bf16[3,6144]{1,0:T(4,128)(2,1)} %param.9, bf16[3,6144]{1,0:T(4,128)(2,1)} %param.8), kind=kLoop, calls=%fused_computation.2 | loop fusion | flops 1916928 | bytes 958464 | tf_op jit(solution)/shard_map/concatenate | solution.py:190
  2.1 0.5 collective-permute-start.1
  2.6 2.6 %collective-permute-start = (f32[32,6144]{1,0:T(8,128)}, f32[32,6144]{1,0:T(8,128)}, u32[]{:S(2)}, u32[]{:S(2)}) collective-permute-start(f32[32,6144]{1,0:T(8,128)} %param.13), channel_id=1, source_target_pairs={{3,0},{0,1},{1,2},{2,3},{7,4},{4,5},{5,6},{6,7},{11,8},{8,9},{9,10... | collective-permute-start | bytes 2359304 | tf_op jit(solution)/shard_map/ppermute | solution.py:182
  5.9 1.1 slice_reduce_fusion
  7.3 0.2 reduce_window_sum.18
  7.5 0.2 fusion.25
  8.1 0.4 fusion.21
  8.7 0.3 broadcast_select_fusion
  9.0 1.6 %collective-permute-start.2 = (bf16[39,6144]{1,0:T(8,128)(2,1)S(1)}, bf16[39,6144]{1,0:T(8,128)(2,1)S(1)}, u32[]{:S(2)}, u32[]{:S(2)}) collective-permute-start(bf16[39,6144]{1,0:T(8,128)(2,1)S(1)} %broadcast_select_fusion), channel_id=1, source_target_pairs={{0,8},{4,12},{8,0},{12,4},{16,24},{20,28},{24,16},{28,20},{1,9},{5... | collective-permute-start | bytes 1437704 | tf_op jit(solution)/shard_map/ppermute | solution.py:174
  10.6 0.5 slice.129
  11.1 1.6 %copy.34 = bf16[32,48,128]{0,2,1:T(8,128)(2,1)} copy(bf16[32,48,128]{2,1,0:T(8,128)(2,1)S(1)} %broadcast_dynamic-update-slice_fusion) | data formatting | bytes 786432 | tf_op jit(solution)/shard_map/stack | solution.py:42
  12.9 9.5 %collective-permute-done.2 = bf16[39,6144]{1,0:T(8,128)(2,1)S(1)} collective-permute-done((bf16[39,6144]{1,0:T(8,128)(2,1)S(1)}, bf16[39,6144]{1,0:T(8,128)(2,1)S(1)}, u32[]{:S(2)}, u32[]{:S(2)}) %collective-permute-start.2) | collective-permute-done | bytes 479264 | tf_op jit(solution)/shard_map/ppermute | solution.py:174
  22.4 1.6 %collective-permute-start.3 = (bf16[39,6144]{1,0:T(8,128)(2,1)S(1)}, bf16[39,6144]{1,0:T(8,128)(2,1)S(1)}, u32[]{:S(2)}, u32[]{:S(2)}) collective-permute-start(bf16[39,6144]{1,0:T(8,128)(2,1)S(1)} %broadcast_select_fusion.1), channel_id=1, source_target_pairs={{0,16},{4,20},{8,24},{12,28},{16,0},{20,4},{24,8},{28,12},{1,17},{... | collective-permute-start | bytes 1437704 | tf_op jit(solution)/shard_map/ppermute | solution.py:174
  24.0 0.3 convert_reduce_fusion.3
  24.3 0.6 shift-left_add_fusion.codes
  24.9 10.2 %collective-permute-done.3 = bf16[39,6144]{1,0:T(8,128)(2,1)S(1)} collective-permute-done((bf16[39,6144]{1,0:T(8,128)(2,1)S(1)}, bf16[39,6144]{1,0:T(8,128)(2,1)S(1)}, u32[]{:S(2)}, u32[]{:S(2)}) %collective-permute-start.3) | collective-permute-done | bytes 479264 | tf_op jit(solution)/shard_map/ppermute | solution.py:174
  35.1 0.1 bitcast_bitcast_fusion
  35.3 0.2 fusion.12
  35.4 0.3 reduce-precision_convert_fusion.8
  36.0 0.2 stack.145
  36.2 0.7 concatenate.17.emit_rows
  37.1 0.7 stack.132
  37.9 0.6 stack.137
  38.6 0.7 stack.135
  39.4 0.1 maximum_bitcast_fusion
  39.5 1.0 copy.35
  40.5 1.1 reshape.100
  41.6 1.1 concatenate.16.em
  42.7 0.8 concatenate.18.rad
  43.5 71.0 %block_term.1 = f32[32,6144]{1,0:T(8,128)} custom-call(s32[1]{0:T(128)} %bitcast.1.count, s32[584]{0:T(1024)} %shift-left_add_fusion.codes, bf16[48,128,32]{2,1,0:T(8,128)(2,1)} %bitcast.67, bf16[49,32,384]{2,1,0:T(8,128)(2,1)} %concatenate.16.em, f32[49,8,128]{2,1,0:T(8,128)} %concatenate.17.emit_rows, bf16[49,32,128]{2,1,0:T(8,128)(2,1)} %concatenate.18.rad), custom_call_target="tpu_custom_call" | custom-call | flops 7549747200 | bytes 8388608 | tf_op jit(solution)/shard_map/block_term/pallas_call | solution.py:152
  114.5 2.3 %multiply_add_fusion = f32[32,6144]{1,0:T(8,128)} fusion(f32[32,6144]{1,0:T(8,128)} %collective-permute-done, f32[32,6144]{1,0:T(8,128)} %block_term.1, f32[6144]{0:T(1024)S(1)} %copy-done.4), kind=kLoop, calls=%fused_computation.1 | loop fusion | flops 393216 | bytes 2383872 | tf_op jit(solution)/shard_map/add | solution.py:200
  (64 shorter events, 1.6 us)
Async XLA Ops:
  0.0 7.2 %copy-start = (s32[48,384]{1,0:T(8,128)S(1)}, s32[48,384]{1,0:T(8,128)}, u32[]{:S(2)}) copy-start(s32[48,384]{1,0:T(8,128)} %param.14) | copy-start | bytes 221188
  0.0 7.0 %copy-start.2 = (bf16[3,6144]{1,0:T(4,128)(2,1)S(1)}, bf16[3,6144]{1,0:T(4,128)(2,1)}, u32[]{:S(2)}) copy-start(bf16[3,6144]{1,0:T(4,128)(2,1)} %param.8) | copy-start | bytes 110596
  0.0 7.1 %copy-start.3 = (bf16[3,6144]{1,0:T(4,128)(2,1)S(1)}, bf16[3,6144]{1,0:T(4,128)(2,1)}, u32[]{:S(2)}) copy-start(bf16[3,6144]{1,0:T(4,128)(2,1)} %param.9) | copy-start | bytes 110596
  0.8 7.9 %copy-start.1 = (bf16[32,6144]{1,0:T(8,128)(2,1)S(1)}, bf16[32,6144]{1,0:T(8,128)(2,1)}, u32[]{:S(2)}) copy-start(bf16[32,6144]{1,0:T(8,128)(2,1)} %param.11) | copy-start | bytes 1179652
  2.1 6.6 %collective-permute-start.1 = (bf16[39,6144]{1,0:T(8,128)(2,1)S(1)}, bf16[39,6144]{1,0:T(8,128)(2,1)S(1)}, u32[]{:S(2)}, u32[]{:S(2)}) collective-permute-start(bf16[39,6144]{1,0:T(8,128)(2,1)S(1)} %pad_maximum_fusion), channel_id=1, source_target_pairs={{0,4},{4,0},{8,12},{12,8},{16,20},{20,16},{24,28},{28,24},{1,5},{5... | collective-permute-start | bytes 1437704 | tf_op jit(solution)/shard_map/ppermute | solution.py:174
  2.6 111.9 %collective-permute-start = (f32[32,6144]{1,0:T(8,128)}, f32[32,6144]{1,0:T(8,128)}, u32[]{:S(2)}, u32[]{:S(2)}) collective-permute-start(f32[32,6144]{1,0:T(8,128)} %param.13), channel_id=1, source_target_pairs={{3,0},{0,1},{1,2},{2,3},{7,4},{4,5},{5,6},{6,7},{11,8},{8,9},{9,10... | collective-permute-start | bytes 2359304 | tf_op jit(solution)/shard_map/ppermute | solution.py:182
  9.0 13.4 %collective-permute-start.2 = (bf16[39,6144]{1,0:T(8,128)(2,1)S(1)}, bf16[39,6144]{1,0:T(8,128)(2,1)S(1)}, u32[]{:S(2)}, u32[]{:S(2)}) collective-permute-start(bf16[39,6144]{1,0:T(8,128)(2,1)S(1)} %broadcast_select_fusion), channel_id=1, source_target_pairs={{0,8},{4,12},{8,0},{12,4},{16,24},{20,28},{24,16},{28,20},{1,9},{5... | collective-permute-start | bytes 1437704 | tf_op jit(solution)/shard_map/ppermute | solution.py:174
  22.4 12.6 %collective-permute-start.3 = (bf16[39,6144]{1,0:T(8,128)(2,1)S(1)}, bf16[39,6144]{1,0:T(8,128)(2,1)S(1)}, u32[]{:S(2)}, u32[]{:S(2)}) collective-permute-start(bf16[39,6144]{1,0:T(8,128)(2,1)S(1)} %broadcast_select_fusion.1), channel_id=1, source_target_pairs={{0,16},{4,20},{8,24},{12,28},{16,0},{20,4},{24,8},{28,12},{1,17},{... | collective-permute-start | bytes 1437704 | tf_op jit(solution)/shard_map/ppermute | solution.py:174
  43.5 71.0 %copy-start.4 = (f32[6144]{0:T(1024)S(1)}, f32[6144]{0:T(1024)}, u32[]{:S(2)}) copy-start(f32[6144]{0:T(1024)} %param.12) | copy-start | bytes 73732
